TPU v7x, 128 devices: a whole 4x4x4 slice. The times are simulated.
128 devices in a mesh: rows: 32 (over y, z, core), cols: 4 (over x).
Axes of the slice: x: 4, y: 4, z: 4, core: 2. Of those that a mesh axis runs over, the one named last changes fastest.
Arguments:
- points: float32 [16, 1048576], P(None, ('rows', 'cols')), may hold values from -2 to 2
- coeffs: float32 [32, 1048576], P(None, ('rows', 'cols')), may hold values from -6 to 6
- velocity: float32 [32, 1048576], P(None, ('rows', 'cols')), may hold values from -4 to 4
- targets: float32 [32, 1048576], P(None, ('rows', 'cols')), may hold values from -6 to 6
- batch_index: int32 [2, 2048], replicated, may hold values from 0 to 1048575, as said below
- test_points: float32 [16, 4096], P(None, 'cols'), may hold values from -2 to 2
Outputs:
- coeffs_out: float32 [32, 1048576], P(None, ('rows', 'cols'))
- velocity_out: float32 [32, 1048576], P(None, ('rows', 'cols'))
- samples: float32 [32, 4096], P(None, 'cols')
Inputs may be any that keep to these rules, and one draw needn't show every extreme that they name: `batch_index`: row numbers of training points, 2048 in each step; a row may repeat within a step, and rows of low-numbered devices are drawn far more often than others.
All inputs are finite; a program needn't handle non-finite values.
Results may differ from a plain program's by a relative error of at most 0.0042.
Values sent between devices are 32-bit elements; how exact they have to be, the bound alone decides.
No kernel may reach another device: no remote copies, remote signals or barrier semaphores. Data moves between devices by JAX's collectives and lax.ppermute only.
A program may use at most 128 MiB of HBM per device.

v0:
```python
import math

import jax
import jax.numpy as jnp
from jax import lax
from jax.sharding import PartitionSpec as P

SCALE = 3.0**0.5 / 1.25


def matern_tile(points_block, queries):
    cross_term = jnp.dot(
        points_block.T, queries, precision=lax.Precision.HIGHEST, preferred_element_type=jnp.float32
    )
    sq_points = jnp.sum(points_block * points_block, axis=0)
    sq_queries = jnp.sum(queries * queries, axis=0)
    dist_sq = jnp.maximum(sq_points[:, None] + sq_queries[None, :] - 2.0 * cross_term, 0.0)
    scaled = SCALE * jnp.sqrt(dist_sq)
    return ((1.0 + scaled) * jnp.exp(-scaled)).astype(jnp.bfloat16)


def kernel_times(points, coeff_half, queries):
    query_count = queries.shape[1]
    blk_width = math.gcd(query_count, 512)
    blocks = queries.reshape(queries.shape[0], query_count // blk_width, blk_width).transpose(
        1, 0, 2
    )

    def apply_block(block):
        return jnp.dot(coeff_half, matern_tile(points, block), preferred_element_type=jnp.float32)

    results = lax.map(apply_block, blocks)
    return results.transpose(1, 0, 2).reshape(coeff_half.shape[0], query_count)


def per_device(points, coeffs, velocity, targets, batch_index, test_points):
    local_count = points.shape[1]
    row_start = lax.axis_index(("rows", "cols")) * local_count

    def take_owned(array, safe_rows, weights):
        return jnp.take(array, safe_rows, axis=1) * weights[None, :]

    steps_total = batch_index.shape[0]
    coeffs_now = coeffs
    velocity_now = velocity
    for step_no in range(steps_total):
        picked = batch_index[step_no]
        offset = picked - row_start
        inside = (offset >= 0) & (offset < local_count)
        owned_safe_rows = jnp.clip(offset, 0, local_count - 1)
        safe_rows = owned_safe_rows
        weights = inside.astype(jnp.float32)
        batch_points = lax.psum(take_owned(points, safe_rows, weights), ("rows", "cols"))
        partial_sums = kernel_times(points, coeffs_now.astype(jnp.bfloat16), batch_points)
        own_terms = take_owned(coeffs_now, safe_rows, weights) * 1.0 - take_owned(
            targets, safe_rows, weights
        )
        gradient = lax.psum(partial_sums + own_terms, ("rows", "cols"))
        summed = jnp.zeros_like(coeffs_now).at[:, safe_rows].add(gradient * weights[None, :])
        velocity_now = 0.9 * velocity_now - 0.5 * summed
        coeffs_now = coeffs_now + velocity_now
    coeff_half = coeffs_now.astype(jnp.bfloat16)
    partial_test = kernel_times(
        points, coeff_half, lax.all_gather(test_points, "cols", axis=1, tiled=True)
    )
    slab_sum = lax.psum_scatter(partial_test, "cols", scatter_dimension=1, tiled=True)
    slab_sum = lax.psum(slab_sum, "rows")
    return (coeffs_now, velocity_now, slab_sum)


def solution(mesh):
    return jax.shard_map(
        per_device,
        mesh=mesh,
        in_specs=(
            P(None, ("rows", "cols")),
            P(None, ("rows", "cols")),
            P(None, ("rows", "cols")),
            P(None, ("rows", "cols")),
            P(),
            P(None, "cols"),
        ),
        out_specs=(P(None, ("rows", "cols")), P(None, ("rows", "cols")), P(None, "cols")),
        check_vma=False,
    )
```

profile of v0, /device:TPU:1, one launch (start us, length us, event | category | flops | bytes accessed | tf_op | source)
XLA Modules:
  0.0 1088.3 jit_solution(15402246799207417307)
XLA Ops:
  8.1 1.4 compare_select_fusion
  9.6 3.5 copy.26
  13.1 9.8 gather_fusion
  22.9 1.7 bitcast_multiply_fusion.7
  25.7 9.8 gather_fusion.3
  35.5 1.7 bitcast_multiply_fusion.4
  37.5 2.6 copy.31
  40.1 3.6 copy.30
  43.7 9.8 gather_fusion.2
  53.6 9.8 gather_fusion.1
  64.4 104.7 %all-reduce.6.cloned.1.call-done = f32[4,16,512]{2,1,0:T(8,128)} async-done(((f32[4,16,512]{2,1,0:T(8,128)}), f32[4,16,512]{2,1,0:T(8,128)}) %all-reduce.6.cloned.1.call-update) | async-done | bytes 131088 | tf_op jit(solution)/shard_map/psum | solution.py:53
  169.1 109.0 %while.36 = (s32[]{:T(128)}, f32[4,32,512]{2,1,0:T(8,128)S(1)}, f32[8192]{0:T(1024)S(1)}, f32[4,16,512]{2,1,0:T(8,128)}, f32[16,8192]{1,0:T(8,128)S(1)}, /*index=5*/bf16[32,8192]{1,0:T(8,128)(2,1)S(1)}, s32[]{:T(128)}) while((s32[]{:T(128)}, f32[4,32,512]{2,1,0:T(8,128)S(1)}, f32[8192]{0:T(1024)S(1)}, f32[4,16,512]{2,1,0:T(8,128)}, ...), condition=%wide.region_4.6_spmd, body=%wide.region_2.5_spmd.sunk | while | flops 1111506432 | bytes 17993824 | solution.py:32
  170.0 23.8 %multiply_convert_fusion.6 = bf16[8192,512]{0,1:T(8,128)(2,1)S(1)} fusion(f32[16,8192]{1,0:T(8,128)S(1)} %get-tuple-element.416, f32[512]{0:T(512)S(1)} %fusion.69, f32[8192]{0:T(1024)S(1)} %get-tuple-element.414, f32[4,16,512]{2,1,0:T(8,128)} %get-tuple-element.415, s32[]{:T(128)S(6)} %copy.59), kind=kOutput, calls=%fused_computation.12.clone.1 | convolution fusion | flops 843055104 | bytes 8980484 | tf_op jit(solution)/shard_map/while/body/eval_jaxpr/dot_general | solution.py:12
  193.8 2.6 fusion.70
  197.2 23.8 %multiply_convert_fusion.6 = bf16[8192,512]{0,1:T(8,128)(2,1)S(1)} fusion(f32[16,8192]{1,0:T(8,128)S(1)} %get-tuple-element.416, f32[512]{0:T(512)S(1)} %fusion.69, f32[8192]{0:T(1024)S(1)} %get-tuple-element.414, f32[4,16,512]{2,1,0:T(8,128)} %get-tuple-element.415, s32[]{:T(128)S(6)} %copy.59), kind=kOutput, calls=%fused_computation.12.clone.1 | convolution fusion | flops 843055104 | bytes 8980484 | tf_op jit(solution)/shard_map/while/body/eval_jaxpr/dot_general | solution.py:12
  221.0 2.6 fusion.70
  224.4 23.8 %multiply_convert_fusion.6 = bf16[8192,512]{0,1:T(8,128)(2,1)S(1)} fusion(f32[16,8192]{1,0:T(8,128)S(1)} %get-tuple-element.416, f32[512]{0:T(512)S(1)} %fusion.69, f32[8192]{0:T(1024)S(1)} %get-tuple-element.414, f32[4,16,512]{2,1,0:T(8,128)} %get-tuple-element.415, s32[]{:T(128)S(6)} %copy.59), kind=kOutput, calls=%fused_computation.12.clone.1 | convolution fusion | flops 843055104 | bytes 8980484 | tf_op jit(solution)/shard_map/while/body/eval_jaxpr/dot_general | solution.py:12
  248.3 2.6 fusion.70
  251.7 23.8 %multiply_convert_fusion.6 = bf16[8192,512]{0,1:T(8,128)(2,1)S(1)} fusion(f32[16,8192]{1,0:T(8,128)S(1)} %get-tuple-element.416, f32[512]{0:T(512)S(1)} %fusion.69, f32[8192]{0:T(1024)S(1)} %get-tuple-element.414, f32[4,16,512]{2,1,0:T(8,128)} %get-tuple-element.415, s32[]{:T(128)S(6)} %copy.59), kind=kOutput, calls=%fused_computation.12.clone.1 | convolution fusion | flops 843055104 | bytes 8980484 | tf_op jit(solution)/shard_map/while/body/eval_jaxpr/dot_general | solution.py:12
  275.5 2.6 fusion.70
  278.4 2.6 fusion.30
  281.4 9.8 gather_fusion.5
  291.2 3.6 copy.25
  294.8 131.6 %all-reduce.12.cloned.1.call-done = (f32[32,2048]{0,1:T(8,128)}, f32[4,16,512]{2,1,0:T(8,128)}) async-done(((f32[32,2048]{0,1:T(8,128)}, f32[4,16,512]{2,1,0:T(8,128)}), (f32[32,2048]{0,1:T(8,128)}, f32[4,16,512]{2,1,0:T(8,128)})) %all-reduce.12.cloned.1.call-update) | async-done | bytes 393232 | tf_op jit(solution)/shard_map/psum | solution.py:58
  426.4 15.7 %scatter_custom_fusion = f32[32,8192]{0,1:T(8,128)} fusion(s32[2048]{0:T(1024)S(1)} %bitcast.194, f32[]{:T(128)} %constant.138.clone.1, f32[32,2048]{0,1:T(8,128)} %get-tuple-element.272, f32[2048]{0:T(1024)S(1)} %bitcast.188), kind=kCustom, calls=%fused_computation.46 | custom fusion | flops 131072 | bytes 1318916 | tf_op jit(solution)/shard_map/scatter-add | solution.py:59
  442.1 7.4 fusion.38
  450.4 102.8 %while.37 = (s32[]{:T(128)}, f32[4,32,512]{2,1,0:T(8,128)S(1)}, f32[8192]{0:T(1024)S(1)}, f32[4,16,512]{2,1,0:T(8,128)S(1)}, f32[16,8192]{1,0:T(8,128)S(1)}, /*index=5*/bf16[32,8192]{1,0:T(8,128)(2,1)S(1)}, s32[]{:T(128)}) while((s32[]{:T(128)}, f32[4,32,512]{2,1,0:T(8,128)S(1)}, f32[8192]{0:T(1024)S(1)}, f32[4,16,512]{2,1,0:T(8,128)S(1)}, ...), condition=%wide.region_10.13_spmd, body=%wide.region_8.12_spmd.sunk | while | flops 1111506432 | bytes 17993824 | solution.py:32
  450.4 23.0 %multiply_convert_fusion.7 = bf16[8192,512]{0,1:T(8,128)(2,1)S(1)} fusion(f32[16,8192]{1,0:T(8,128)S(1)} %get-tuple-element.437, f32[512]{0:T(512)S(1)} %fusion.75, f32[8192]{0:T(1024)S(1)} %get-tuple-element.435, f32[4,16,512]{2,1,0:T(8,128)S(1)} %get-tuple-element.436, s32[]{:T(128)S(6)} %copy.67), kind=kOutput, calls=%fused_computation.24.clone.1 | convolution fusion | flops 843055104 | bytes 8980484 | tf_op jit(solution)/shard_map/while/body/eval_jaxpr/dot_general | solution.py:12
  473.5 2.6 fusion.76
  476.1 23.1 %multiply_convert_fusion.7 = bf16[8192,512]{0,1:T(8,128)(2,1)S(1)} fusion(f32[16,8192]{1,0:T(8,128)S(1)} %get-tuple-element.437, f32[512]{0:T(512)S(1)} %fusion.75, f32[8192]{0:T(1024)S(1)} %get-tuple-element.435, f32[4,16,512]{2,1,0:T(8,128)S(1)} %get-tuple-element.436, s32[]{:T(128)S(6)} %copy.67), kind=kOutput, calls=%fused_computation.24.clone.1 | convolution fusion | flops 843055104 | bytes 8980484 | tf_op jit(solution)/shard_map/while/body/eval_jaxpr/dot_general | solution.py:12
  499.2 2.6 fusion.76
  501.8 23.1 %multiply_convert_fusion.7 = bf16[8192,512]{0,1:T(8,128)(2,1)S(1)} fusion(f32[16,8192]{1,0:T(8,128)S(1)} %get-tuple-element.437, f32[512]{0:T(512)S(1)} %fusion.75, f32[8192]{0:T(1024)S(1)} %get-tuple-element.435, f32[4,16,512]{2,1,0:T(8,128)S(1)} %get-tuple-element.436, s32[]{:T(128)S(6)} %copy.67), kind=kOutput, calls=%fused_computation.24.clone.1 | convolution fusion | flops 843055104 | bytes 8980484 | tf_op jit(solution)/shard_map/while/body/eval_jaxpr/dot_general | solution.py:12
  524.9 2.6 fusion.76
  527.5 23.1 %multiply_convert_fusion.7 = bf16[8192,512]{0,1:T(8,128)(2,1)S(1)} fusion(f32[16,8192]{1,0:T(8,128)S(1)} %get-tuple-element.437, f32[512]{0:T(512)S(1)} %fusion.75, f32[8192]{0:T(1024)S(1)} %get-tuple-element.435, f32[4,16,512]{2,1,0:T(8,128)S(1)} %get-tuple-element.436, s32[]{:T(128)S(6)} %copy.67), kind=kOutput, calls=%fused_computation.24.clone.1 | convolution fusion | flops 843055104 | bytes 8980484 | tf_op jit(solution)/shard_map/while/body/eval_jaxpr/dot_general | solution.py:12
  550.6 2.6 fusion.76
  553.5 9.8 gather_fusion.4
  563.4 2.6 fusion.27
  566.0 19.5 %all_gather.3 = f32[16,4096]{1,0:T(8,128)S(1)} all-gather(f32[16,1024]{1,0:T(8,128)S(1)} %copy-done.7), channel_id=1, replica_groups=mesh['rows'=32,'cols'=4] {'cols'}, dimensions={1}, use_global_device_ids=true | all-gather | bytes 327680 | tf_op jit(solution)/shard_map/all_gather | solution.py:64
  585.7 129.1 %all-reduce.8.cloned.1.call-done = f32[32,2048]{0,1:T(8,128)} async-done(((f32[32,2048]{0,1:T(8,128)}), f32[32,2048]{0,1:T(8,128)}) %all-reduce.8.cloned.1.call-update) | async-done | bytes 262160 | tf_op jit(solution)/shard_map/psum | solution.py:58
  714.8 15.8 %scatter_custom_fusion.1 = f32[32,8192]{0,1:T(8,128)} fusion(s32[2048]{0:T(1024)} %bitcast.193, f32[]{:T(128)} %constant.138.clone.1, f32[32,2048]{0,1:T(8,128)} %all-reduce.8.cloned.1.call-done, f32[2048]{0:T(1024)S(1)} %bitcast.185), kind=kCustom, calls=%fused_computation.44 | custom fusion | flops 131072 | bytes 2105856 | tf_op jit(solution)/shard_map/scatter-add | solution.py:59
  730.6 10.3 fusion.37
  741.7 210.7 %while.38 = (s32[]{:T(128)}, f32[8,32,512]{2,1,0:T(8,128)}, f32[8192]{0:T(1024)S(1)}, f32[8,16,512]{2,0,1:T(8,128)S(1)}, f32[16,8192]{1,0:T(8,128)S(1)}, /*index=5*/bf16[32,8192]{1,0:T(8,128)(2,1)S(1)}, s32[]{:T(128)}) while((s32[]{:T(128)}, f32[8,32,512]{2,1,0:T(8,128)}, f32[8192]{0:T(1024)S(1)}, f32[8,16,512]{2,0,1:T(8,128)S(1)}, ...), condition=%wide.region_15.18_spmd, body=%wide.region_13.17_spmd.sunk | while | flops 1111506432 | bytes 18059356 | solution.py:32
  741.8 23.0 %multiply_convert_fusion.8 = bf16[8192,512]{0,1:T(8,128)(2,1)S(1)} fusion(f32[16,8192]{1,0:T(8,128)S(1)} %get-tuple-element.458, f32[512]{0:T(512)S(1)} %multiply_reduce_fusion.3, f32[8192]{0:T(1024)S(1)} %get-tuple-element.456, f32[1,16,512]{2,0,1:T(1,128)S(1)} %constant_dynamic-slice_fusion.2), kind=kOutput, calls=%fused_computation.36.clone.1 | convolution fusion | flops 843055104 | bytes 8980480 | tf_op jit(solution)/shard_map/while/body/eval_jaxpr/dot_general | solution.py:12
  764.8 3.2 fusion.80
  768.1 23.0 %multiply_convert_fusion.8 = bf16[8192,512]{0,1:T(8,128)(2,1)S(1)} fusion(f32[16,8192]{1,0:T(8,128)S(1)} %get-tuple-element.458, f32[512]{0:T(512)S(1)} %multiply_reduce_fusion.3, f32[8192]{0:T(1024)S(1)} %get-tuple-element.456, f32[1,16,512]{2,0,1:T(1,128)S(1)} %constant_dynamic-slice_fusion.2), kind=kOutput, calls=%fused_computation.36.clone.1 | convolution fusion | flops 843055104 | bytes 8980480 | tf_op jit(solution)/shard_map/while/body/eval_jaxpr/dot_general | solution.py:12
  791.2 3.2 fusion.80
  794.5 23.0 %multiply_convert_fusion.8 = bf16[8192,512]{0,1:T(8,128)(2,1)S(1)} fusion(f32[16,8192]{1,0:T(8,128)S(1)} %get-tuple-element.458, f32[512]{0:T(512)S(1)} %multiply_reduce_fusion.3, f32[8192]{0:T(1024)S(1)} %get-tuple-element.456, f32[1,16,512]{2,0,1:T(1,128)S(1)} %constant_dynamic-slice_fusion.2), kind=kOutput, calls=%fused_computation.36.clone.1 | convolution fusion | flops 843055104 | bytes 8980480 | tf_op jit(solution)/shard_map/while/body/eval_jaxpr/dot_general | solution.py:12
  817.5 3.2 fusion.80
  820.8 23.0 %multiply_convert_fusion.8 = bf16[8192,512]{0,1:T(8,128)(2,1)S(1)} fusion(f32[16,8192]{1,0:T(8,128)S(1)} %get-tuple-element.458, f32[512]{0:T(512)S(1)} %multiply_reduce_fusion.3, f32[8192]{0:T(1024)S(1)} %get-tuple-element.456, f32[1,16,512]{2,0,1:T(1,128)S(1)} %constant_dynamic-slice_fusion.2), kind=kOutput, calls=%fused_computation.36.clone.1 | convolution fusion | flops 843055104 | bytes 8980480 | tf_op jit(solution)/shard_map/while/body/eval_jaxpr/dot_general | solution.py:12
  843.9 3.2 fusion.80
  847.2 23.0 %multiply_convert_fusion.8 = bf16[8192,512]{0,1:T(8,128)(2,1)S(1)} fusion(f32[16,8192]{1,0:T(8,128)S(1)} %get-tuple-element.458, f32[512]{0:T(512)S(1)} %multiply_reduce_fusion.3, f32[8192]{0:T(1024)S(1)} %get-tuple-element.456, f32[1,16,512]{2,0,1:T(1,128)S(1)} %constant_dynamic-slice_fusion.2), kind=kOutput, calls=%fused_computation.36.clone.1 | convolution fusion | flops 843055104 | bytes 8980480 | tf_op jit(solution)/shard_map/while/body/eval_jaxpr/dot_general | solution.py:12
  870.2 3.2 fusion.80
  873.5 23.0 %multiply_convert_fusion.8 = bf16[8192,512]{0,1:T(8,128)(2,1)S(1)} fusion(f32[16,8192]{1,0:T(8,128)S(1)} %get-tuple-element.458, f32[512]{0:T(512)S(1)} %multiply_reduce_fusion.3, f32[8192]{0:T(1024)S(1)} %get-tuple-element.456, f32[1,16,512]{2,0,1:T(1,128)S(1)} %constant_dynamic-slice_fusion.2), kind=kOutput, calls=%fused_computation.36.clone.1 | convolution fusion | flops 843055104 | bytes 8980480 | tf_op jit(solution)/shard_map/while/body/eval_jaxpr/dot_general | solution.py:12
  896.5 3.2 fusion.80
  899.8 23.0 %multiply_convert_fusion.8 = bf16[8192,512]{0,1:T(8,128)(2,1)S(1)} fusion(f32[16,8192]{1,0:T(8,128)S(1)} %get-tuple-element.458, f32[512]{0:T(512)S(1)} %multiply_reduce_fusion.3, f32[8192]{0:T(1024)S(1)} %get-tuple-element.456, f32[1,16,512]{2,0,1:T(1,128)S(1)} %constant_dynamic-slice_fusion.2), kind=kOutput, calls=%fused_computation.36.clone.1 | convolution fusion | flops 843055104 | bytes 8980480 | tf_op jit(solution)/shard_map/while/body/eval_jaxpr/dot_general | solution.py:12
  922.9 3.2 fusion.80
  926.2 23.0 %multiply_convert_fusion.8 = bf16[8192,512]{0,1:T(8,128)(2,1)S(1)} fusion(f32[16,8192]{1,0:T(8,128)S(1)} %get-tuple-element.458, f32[512]{0:T(512)S(1)} %multiply_reduce_fusion.3, f32[8192]{0:T(1024)S(1)} %get-tuple-element.456, f32[1,16,512]{2,0,1:T(1,128)S(1)} %constant_dynamic-slice_fusion.2), kind=kOutput, calls=%fused_computation.36.clone.1 | convolution fusion | flops 843055104 | bytes 8980480 | tf_op jit(solution)/shard_map/while/body/eval_jaxpr/dot_general | solution.py:12
  949.2 3.2 fusion.80
  952.5 1.9 copy.43
  954.4 20.8 %reduce-scatter.2.cloned.1.call-done = f32[32,1024]{1,0:T(8,128)} async-done(((f32[32,4096]{1,0:T(8,128)}), f32[32,1024]{1,0:T(8,128)}) %reduce-scatter.2.cloned.1.call-update) | async-done | bytes 131088 | tf_op jit(solution)/shard_map/reduce_scatter | solution.py:66
  975.3 3.6 copy.40
  978.9 3.6 copy.41
  982.5 97.5 %all-reduce.10.cloned.1.call-done = f32[32,1024]{1,0:T(8,128)} async-done(((f32[32,1024]{1,0:T(8,128)}), f32[32,1024]{1,0:T(8,128)}) %all-reduce.10.cloned.1.call-update) | async-done | bytes 131088 | tf_op jit(solution)/shard_map/psum | solution.py:67
  1080.0 1.6 copy.83
  (71 shorter events, 9.8 us)
Async XLA Ops:
  7.2 30.1 %copy-start.1 = (f32[16,8192]{1,0:T(8,128)S(1)}, f32[16,8192]{1,0:T(8,128)}, u32[]{:S(2)}) copy-start(f32[16,8192]{1,0:T(8,128)} %param.16) | copy-start | bytes 1572868
  7.2 30.2 %copy-start = (f32[32,8192]{1,0:T(8,128)S(1)}, f32[32,8192]{1,0:T(8,128)}, u32[]{:S(2)}) copy-start(f32[32,8192]{1,0:T(8,128)} %param.17) | copy-start | bytes 3145732
  7.2 161.9 %all-reduce.6.cloned.1.call-start = ((), (), s32[]{:S(2)}) async-start(), calls=%async_computation.1 | async-start | bytes 262144 | tf_op jit(solution)/shard_map/psum | solution.py:53
  8.1 29.2 %copy-start.5 = (f32[1,2048]{1,0:T(1,128)}, f32[1,2048]{1,0:T(1,128)S(1)}, u32[]{:S(2)}) copy-start(f32[1,2048]{1,0:T(1,128)S(1)} %get-tuple-element.283) | copy-start | bytes 24580
  25.6 400.8 %all-reduce.12.cloned.1.call-start = ((), (), s32[]{:S(2)}) async-start(), calls=%async_computation.5 | async-start | bytes 2359296 | tf_op jit(solution)/shard_map/psum | solution.py:58
  25.7 27.9 %copy-start.8 = (pred[2048]{0:T(1024)(128)(4,1)}, pred[2048]{0:T(1024)(128)(4,1)S(1)}, u32[]{:S(2)}) copy-start(pred[2048]{0:T(1024)(128)(4,1)S(1)} %compare_and_fusion) | copy-start | bytes 6148
  169.1 109.4 %copy-start.3 = (f32[2048,32]{1,0:T(8,128)S(1)}, f32[2048,32]{1,0:T(8,128)}, u32[]{:S(2)}) copy-start(f32[2048,32]{1,0:T(8,128)} %gather_fusion.2) | copy-start | bytes 786436
  281.0 433.8 %all-reduce.8.cloned.1.call-start = ((), (), s32[]{:S(2)}) async-start(), calls=%async_computation.2 | async-start | bytes 2097152 | tf_op jit(solution)/shard_map/psum | solution.py:58
  442.1 8.3 copy-start.4
  450.3 113.0 %copy-start.2 = (f32[2048,32]{1,0:T(8,128)S(1)}, f32[2048,32]{1,0:T(8,128)}, u32[]{:S(2)}) copy-start(f32[2048,32]{1,0:T(8,128)} %gather_fusion.5) | copy-start | bytes 786436
  450.4 113.0 %copy-start.6 = (f32[1,2048]{1,0:T(1,128)S(1)}, f32[1,2048]{1,0:T(1,128)}, u32[]{:S(2)}) copy-start(f32[1,2048]{1,0:T(1,128)} %copy-done.5) | copy-start | bytes 24580
  450.4 113.0 %copy-start.9 = (pred[2048]{0:T(1024)(128)(4,1)S(1)}, pred[2048]{0:T(1024)(128)(4,1)}, u32[]{:S(2)}) copy-start(pred[2048]{0:T(1024)(128)(4,1)} %copy-done.8) | copy-start | bytes 6148
  553.2 12.9 %copy-start.7 = (f32[16,1024]{1,0:T(8,128)S(1)}, f32[16,1024]{1,0:T(8,128)}, u32[]{:S(2)}) copy-start(f32[16,1024]{1,0:T(8,128)} %param.21) | copy-start | bytes 196612
  566.0 409.3 %reduce-scatter.2.cloned.1.call-start = ((), (), s32[]{:S(2)}) async-start(), calls=%async_computation.3 | async-start | bytes 655360 | tf_op jit(solution)/shard_map/reduce_scatter | solution.py:66
  954.4 125.6 %all-reduce.10.cloned.1.call-start = ((), (), s32[]{:S(2)}) async-start(), calls=%async_computation.4 | async-start | bytes 262144 | tf_op jit(solution)/shard_map/psum | solution.py:67
Sparse Core Ops, SparseCore 0:
  25.7 143.2 all-reduce.5
  281.2 145.1 all-reduce.11
  566.1 148.6 all-reduce.7
  954.5 20.7 reduce-scatter.1
  978.7 101.2 all-reduce.9
where the time goes:
time: 1100 us; the launch traced here: 1090 us
  waiting for transfers between devices  484 us (44%)
  matrix products  419 us (38%)
  local copies, waits for them, and re-layouts  87.6 us (8%)
  other arithmetic  63.9 us (6%)
  blocking collectives  19.5 us (2%)
  between operations  14.2 us (1%)
    dot_general x16, matrix products, matern_tile(): jnp.dot(points_block.T, queries, precision=lax.Precision.HIGHEST, preferr...  372 us
    psum x2, waiting for transfers between devices, per_device(): gradient = lax.psum(partial_sums + own_terms, ('rows', 'cols'))  261 us
    psum x1, waiting for transfers between devices, per_device(): lax.psum(take_owned(points, safe_rows, weights), ('rows', 'cols'))  105 us
    psum x1, waiting for transfers between devices, per_device(): slab_sum = lax.psum(slab_sum, 'rows')  97.5 us
    gather x6, local copies, waits for them, and re-layouts, take_owned(): return jnp.take(array, safe_rows, axis=1) * weights[None, :]  58.9 us
    dot_general x16, matrix products, apply_block(): jnp.dot(coeff_half, matern_tile(points, block), preferred_element_type=jn...  46.8 us
    scatter-add x2, other arithmetic, per_device(): jnp.zeros_like(coeffs_now).at[:, safe_rows].add(gradient * weights[None, :])  31.5 us
    unnamed x28, local copies, waits for them, and re-layouts  22.4 us
  transfers between devices with their start and end apart: 5, of which 5 were waited for; matrix products, arithmetic and copies ran while one was open for 5% of the time, Pallas kernels for 0%

commit v1 on v0

v1 whole, which is shorter than its diff:
```python
import functools
import math

import jax
import jax.numpy as jnp
from jax import lax
from jax.experimental import pallas as pl
from jax.experimental.pallas import tpu as pltpu
from jax.sharding import PartitionSpec as P

BOTH = ("rows", "cols")
SCALE = 3.0**0.5 / 1.25
UNIT = SCALE / math.log(2.0)
SHIFT = 1.0 / math.log(2.0)
DROP = math.log2(math.log(2.0))
DEPTH = 128
WIDE = 256
F32 = jnp.float32
BF16 = jnp.bfloat16
VMEM_LIMIT = 48 << 20


def split(x, parts):
    pieces = []
    for _ in range(parts - 1):
        piece = x.astype(BF16)
        pieces.append(piece)
        x = x - piece.astype(F32)
    pieces.append(x.astype(BF16))
    return pieces


def tail_rows(norm_sq, norms_first):
    row = lax.broadcasted_iota(jnp.int32, (16, norm_sq.shape[1]), 0)
    base, ones = (0, 3) if norms_first else (3, 0)
    out = jnp.where((row >= ones) & (row < ones + 3), 1.0, 0.0)
    rest = norm_sq
    for piece_no in range(3):
        piece = rest.astype(BF16).astype(F32)
        out = jnp.where(row == base + piece_no, piece, out)
        rest = rest - piece
    return out.astype(BF16)


def point_side(points):
    x = points * UNIT
    a, b, c = split(x, 3)
    tail = tail_rows(jnp.sum(x * x, axis=0, keepdims=True), True)
    return jnp.concatenate([a, a, b, a, b, c, b, tail], axis=0)


def query_side(queries):
    x = queries * UNIT
    a, b, c = split(-2.0 * x, 3)
    tail = tail_rows(jnp.sum(x * x, axis=0, keepdims=True), False)
    return jnp.concatenate([a, b, a, c, b, a, c, tail], axis=0)


def transposed(x):
    return x.astype(F32).T.astype(BF16)


def matern(u_sq):
    u_sq = jnp.maximum(u_sq, 1e-12)
    u = u_sq * lax.rsqrt(u_sq)
    return (u + SHIFT) * jnp.exp2(DROP - u)


def last_dims(a, b):
    return lax.dot_general(a, b, (((1,), (1,)), ((), ())), preferred_element_type=F32)


def params():
    return pltpu.CompilerParams(vmem_limit_bytes=VMEM_LIMIT)


def cost(evaluations):
    return pl.CostEstimate(
        flops=evaluations * 1024, bytes_accessed=1 << 20, transcendentals=2 * evaluations
    )


def store_tiles(out_ref, value, lead):
    rows, columns = value.shape
    high = out_ref.shape[-2]
    for i in range(rows // high):
        for j in range(columns // 128):
            out_ref[lead(i, j)] = value[i * high : (i + 1) * high, j * 128 : (j + 1) * 128]


def prepare_kernel(points, coeffs, velocity, sides, halves):
    sides[...] = point_side(points[...])
    c = coeffs[...]
    halves[0] = c.astype(BF16)
    v = 0.9 * velocity[...]
    c = c + v
    halves[1] = c.astype(BF16)
    halves[2] = (c + 0.9 * v).astype(BF16)


def prepare(points, coeffs, velocity):
    feats, count = points.shape
    samples = coeffs.shape[0]
    blk = min(count, 1024)
    return pl.pallas_call(
        prepare_kernel,
        grid=(count // blk,),
        in_specs=[
            pl.BlockSpec((feats, blk), lambda i: (0, i)),
            pl.BlockSpec((samples, blk), lambda i: (0, i)),
            pl.BlockSpec((samples, blk), lambda i: (0, i)),
        ],
        out_specs=[
            pl.BlockSpec((DEPTH, blk), lambda i: (0, i)),
            pl.BlockSpec((3, samples, blk), lambda i: (0, 0, i)),
        ],
        out_shape=[
            jax.ShapeDtypeStruct((DEPTH, count), BF16),
            jax.ShapeDtypeStruct((3, samples, count), BF16),
        ],
        compiler_params=params(),
        name="prepare",
    )(points, coeffs, velocity)


def select_owned(stack, local, rows, parts):
    blocks = stack.shape[0] // rows
    q = local.shape[1]
    low = jnp.bitwise_and(local, WIDE - 1)
    high = jnp.right_shift(local, WIDE.bit_length() - 1)
    hot = (lax.broadcasted_iota(jnp.int32, (WIDE, q), 0) == low).astype(F32).astype(BF16)
    picked = jnp.dot(
        stack[...], jnp.concatenate([hot] * parts, axis=0), preferred_element_type=F32
    )
    total = jnp.zeros((rows, q), F32)
    for block in range(blocks):
        total = total + jnp.where(high == block, picked[block * rows : (block + 1) * rows], 0.0)
    return total


def fill_stack(stack, value_of, rows, parts):
    for block in range(stack.shape[0] // rows):
        pieces = split(value_of(slice(block * WIDE, (block + 1) * WIDE)), parts)
        for part, piece in enumerate(pieces):
            stack[block * rows : (block + 1) * rows, part * WIDE : (part + 1) * WIDE] = piece


def gather_points_kernel(start, index, points, out, stack):
    rows = points.shape[0]

    @pl.when(pl.program_id(0) == 0)
    def _():
        fill_stack(stack, lambda cols: points[:, cols], rows, 3)

    got = select_owned(stack, index[0] - start[0], rows, 3)
    store_tiles(out, got, lambda i, j: (i, j))


def gather_points(start, index, points):
    feats, count = points.shape
    steps, _, blk = index.shape
    return pl.pallas_call(
        gather_points_kernel,
        grid=(steps,),
        in_specs=[
            pl.BlockSpec(memory_space=pltpu.SMEM),
            pl.BlockSpec((1, 1, blk), lambda i: (i, 0, 0)),
            pl.BlockSpec((feats, count), lambda i: (0, 0)),
        ],
        out_specs=pl.BlockSpec((feats // 4, blk // 128, 4, 128), lambda i: (0, i, 0, 0)),
        out_shape=jax.ShapeDtypeStruct((feats // 4, steps * blk // 128, 4, 128), F32),
        scratch_shapes=[pltpu.VMEM((count // WIDE * feats, 3 * WIDE), BF16)],
        compiler_params=params(),
        name="gather_points",
    )(start, index, points)


def gather_terms_kernel(half_steps, start, index, coeffs, velocity, targets, out, stack):
    rows = coeffs.shape[0]

    @pl.when(pl.program_id(0) == 0)
    def _():
        fill_stack(stack, lambda cols: coeffs[:, cols] - targets[:, cols], rows, 2)

    @pl.when(pl.program_id(0) == half_steps)
    def _():
        fill_stack(
            stack,
            lambda cols: coeffs[:, cols] + 0.9 * velocity[:, cols] - targets[:, cols],
            rows,
            2,
        )

    got = select_owned(stack, index[0] - start[0], rows, 2)
    store_tiles(out, got, lambda i, j: (i, j))


def gather_terms(start, index, coeffs, velocity, targets):
    samples, count = coeffs.shape
    steps, _, blk = index.shape
    whole = pl.BlockSpec((samples, count), lambda i: (0, 0))
    return pl.pallas_call(
        functools.partial(gather_terms_kernel, steps // 2),
        grid=(steps,),
        in_specs=[
            pl.BlockSpec(memory_space=pltpu.SMEM),
            pl.BlockSpec((1, 1, blk), lambda i: (i, 0, 0)),
            whole,
            whole,
            whole,
        ],
        out_specs=pl.BlockSpec((samples // 8, blk // 128, 8, 128), lambda i: (0, i, 0, 0)),
        out_shape=jax.ShapeDtypeStruct((samples // 8, steps * blk // 128, 8, 128), F32),
        scratch_shapes=[pltpu.VMEM((count // WIDE * samples, 2 * WIDE), BF16)],
        compiler_params=params(),
        name="gather_terms",
    )(start, index, coeffs, velocity, targets)


def kernel_sums(side_t, sides, halves, chunk, unroll):
    count = sides.shape[1]
    q = side_t.shape[0]

    def step(i, acc):
        cols = pl.ds(pl.multiple_of(i * chunk, chunk), chunk)
        u_sq = jnp.dot(side_t[...], sides[:, cols], preferred_element_type=F32)
        return acc + last_dims(halves[:, cols], matern(u_sq).astype(BF16))

    return lax.fori_loop(
        0, count // chunk, step, jnp.zeros((halves.shape[0], q), F32), unroll=unroll
    )


def batch_kernel(queries, sides, halves, terms, out, side_t):
    side_t[...] = transposed(query_side(queries[...]))
    total = kernel_sums(side_t, sides, halves.at[0], 256, 16)
    for i in range(out.shape[0]):
        for j in range(out.shape[1]):
            out[i, j] = (
                total[i * 8 : (i + 1) * 8, j * 128 : (j + 1) * 128] + terms[i, j]
            )


def batch_sums(queries, sides, halves, terms):
    feats, total = queries.shape
    _, samples, count = halves.shape
    blk = 512
    steps = total // blk
    tile = pl.BlockSpec((samples // 8, blk // 128, 8, 128), lambda i: (0, i, 0, 0))
    return pl.pallas_call(
        batch_kernel,
        grid=(steps,),
        in_specs=[
            pl.BlockSpec((feats, blk), lambda i: (0, i)),
            pl.BlockSpec((DEPTH, count), lambda i: (0, 0)),
            pl.BlockSpec((1, samples, count), lambda i: (i // (steps // 2), 0, 0)),
            tile,
        ],
        out_specs=tile,
        out_shape=jax.ShapeDtypeStruct(terms.shape, F32),
        scratch_shapes=[pltpu.VMEM((blk, DEPTH), BF16)],
        compiler_params=params(),
        cost_estimate=cost(total * count),
        name="batch_sums",
    )(queries, sides, halves, terms)


def test_kernel(queries, sides, halves, *refs):
    out, side_t = refs[-2:]
    side_t[...] = transposed(query_side(queries[...]))
    total = kernel_sums(side_t, sides, halves.at[0], 256, 16)
    store_tiles(out, total, lambda i, j: (i, j, 0))


def test_sums(slab, n_slabs, queries, sides, halves, before):
    feats, total = queries.shape
    _, samples, count = halves.shape
    blk = 512
    per_slab = total // n_slabs
    steps = per_slab // blk
    in_specs = [
        pl.BlockSpec((feats, blk), lambda i: (0, slab * steps + i)),
        pl.BlockSpec((DEPTH, count), lambda i: (0, 0)),
        pl.BlockSpec((1, samples, count), lambda i: (2, 0, 0)),
    ]
    args = [queries, sides, halves]
    aliases = {}
    if before is not None:
        in_specs.append(pl.BlockSpec(memory_space=pl.ANY))
        args.append(before)
        aliases = {3: 0}
    return pl.pallas_call(
        test_kernel,
        grid=(steps,),
        in_specs=in_specs,
        out_specs=pl.BlockSpec(
            (samples // 8, blk // 128, 1, 8, 128), lambda i: (0, i, slab, 0, 0)
        ),
        out_shape=jax.ShapeDtypeStruct((samples // 8, per_slab // 128, n_slabs, 8, 128), F32),
        scratch_shapes=[pltpu.VMEM((blk, DEPTH), BF16)],
        input_output_aliases=aliases,
        compiler_params=params(),
        cost_estimate=cost(per_slab * count),
        name="test_sums",
    )(*args)


def second_kernel(queries, first, index0, index1, grad, sums, out, sides, weights, side_t, col):
    @pl.when(pl.program_id(0) == 0)
    def _():
        sides[...] = point_side(first[...])
        high, low = split(-0.5 * grad[...], 2)
        weights[...] = jnp.concatenate([high, low], axis=0)

    side_t[...] = transposed(query_side(queries[...]))
    blk = queries.shape[1]
    col[...] = jnp.broadcast_to(index1[0].astype(F32), (128, blk)).T
    chunk = 256

    def step(i, acc):
        cols = pl.ds(pl.multiple_of(i * chunk, chunk), chunk)
        u_sq = jnp.dot(side_t[...], sides[:, cols], preferred_element_type=F32)
        there = jnp.concatenate([col[...]] * (chunk // 128), axis=1)
        same = there == index0[0:1, cols].astype(F32)
        kern = matern(u_sq) + jnp.where(same, 1.0, 0.0)
        return acc + last_dims(weights[:, cols], kern.astype(BF16))

    total = lax.fori_loop(
        0, sides.shape[1] // chunk, step, jnp.zeros((weights.shape[0], blk), F32), unroll=True
    )
    half = weights.shape[0] // 2
    out[...] = sums[...] + total[:half] + total[half:]


def second_gradient(drawn, index, index_blocks, grad, sums):
    feats, total = drawn.shape
    samples, batch = grad.shape
    blk = 512
    steps = batch // blk
    return pl.pallas_call(
        second_kernel,
        grid=(steps,),
        in_specs=[
            pl.BlockSpec((feats, blk), lambda i: (0, steps + i)),
            pl.BlockSpec((feats, batch), lambda i: (0, 0)),
            pl.BlockSpec((2, batch), lambda i: (0, 0)),
            pl.BlockSpec((1, 1, blk), lambda i: (steps + i, 0, 0)),
            pl.BlockSpec((samples, batch), lambda i: (0, 0)),
            pl.BlockSpec((samples, blk), lambda i: (0, i)),
        ],
        out_specs=pl.BlockSpec((samples, blk), lambda i: (0, i)),
        out_shape=jax.ShapeDtypeStruct((samples, batch), F32),
        scratch_shapes=[
            pltpu.VMEM((DEPTH, batch), BF16),
            pltpu.VMEM((2 * samples, batch), BF16),
            pltpu.VMEM((blk, DEPTH), BF16),
            pltpu.VMEM((blk, 128), F32),
        ],
        compiler_params=params(),
        cost_estimate=cost(batch * batch),
        name="second_gradient",
    )(drawn, drawn, index, index_blocks, grad, sums)


def test_change_kernel(queries, drawn, grad0, grad1, out, sides, weights, side_t):
    batch = grad0.shape[1]

    @pl.when(pl.program_id(0) == 0)
    def _():
        sides[...] = point_side(drawn[...])
        for no, (grad, factor) in enumerate(((grad0, -0.95), (grad1, -0.5))):
            high, low = split(factor * grad[...], 2)
            weights[:, no * batch : (no + 1) * batch] = jnp.concatenate([high, low], axis=0)

    side_t[...] = transposed(query_side(queries[...]))
    total = kernel_sums(side_t, sides, weights, 256, True)
    half = weights.shape[0] // 2
    out[...] = total[:half] + total[half:]


def test_change(queries, drawn, grad0, grad1):
    feats, slab = queries.shape
    samples, batch = grad0.shape
    total = drawn.shape[1]
    blk = 512
    return pl.pallas_call(
        test_change_kernel,
        grid=(slab // blk,),
        in_specs=[
            pl.BlockSpec((feats, blk), lambda i: (0, i)),
            pl.BlockSpec((feats, total), lambda i: (0, 0)),
            pl.BlockSpec((samples, batch), lambda i: (0, 0)),
            pl.BlockSpec((samples, batch), lambda i: (0, 0)),
        ],
        out_specs=pl.BlockSpec((samples, blk), lambda i: (0, i)),
        out_shape=jax.ShapeDtypeStruct((samples, slab), F32),
        scratch_shapes=[
            pltpu.VMEM((DEPTH, total), BF16),
            pltpu.VMEM((2 * samples, total), BF16),
            pltpu.VMEM((blk, DEPTH), BF16),
        ],
        compiler_params=params(),
        cost_estimate=cost(total * slab),
        name="test_change",
    )(queries, drawn, grad0, grad1)


def update_kernel(
    start, index, coeffs, velocity, grad0, grad1, coeffs_out, velocity_out, hot, pieces, masked
):
    samples, batch = grad0.shape
    block_cols = coeffs.shape[1] // WIDE
    local = index[...] - start[0]
    high = jnp.right_shift(local, WIDE.bit_length() - 1)

    @pl.when(pl.program_id(0) == 0)
    def _():
        low = jnp.bitwise_and(local, WIDE - 1).astype(F32)
        lane = lax.broadcasted_iota(jnp.int32, (batch, 128), 1).astype(F32)
        for step, grad in enumerate((grad0, grad1)):
            column = jnp.broadcast_to(low[step : step + 1], (128, batch)).T
            for part in range(WIDE // 128):
                hot[step, :, part * 128 : (part + 1) * 128] = (
                    (column == lane + part * 128.0).astype(F32).astype(BF16)
                )
            first, second = split(grad[...], 2)
            pieces[step, :samples] = first
            pieces[step, samples:] = second

    first_block = pl.program_id(0) * block_cols
    sums = []
    for step in range(2):
        for block in range(block_cols):
            here = (high[step : step + 1] == first_block + block).astype(F32)
            here = jnp.broadcast_to(here, (16, batch)).astype(BF16)
            for part in range(2 * samples // 16):
                row = block * 2 * samples + part * 16
                masked[row : row + 16] = pieces[step, part * 16 : (part + 1) * 16] * here
        sums.append(jnp.dot(masked[...], hot[step], preferred_element_type=F32))
    for block in range(block_cols):
        cols = slice(block * WIDE, (block + 1) * WIDE)
        top = block * 2 * samples
        g0, g1 = (s[top : top + samples] + s[top + samples : top + 2 * samples] for s in sums)
        v1 = 0.9 * velocity[:, cols] - 0.5 * g0
        c1 = coeffs[:, cols] + v1
        v2 = 0.9 * v1 - 0.5 * g1
        velocity_out[:, cols] = v2
        coeffs_out[:, cols] = c1 + v2


def update(start, index, coeffs, velocity, grad0, grad1):
    samples, count = coeffs.shape
    batch = grad0.shape[1]
    blk = min(count, 2048)
    return pl.pallas_call(
        update_kernel,
        grid=(count // blk,),
        in_specs=[
            pl.BlockSpec(memory_space=pltpu.SMEM),
            pl.BlockSpec((2, batch), lambda i: (0, 0)),
            pl.BlockSpec((samples, blk), lambda i: (0, i)),
            pl.BlockSpec((samples, blk), lambda i: (0, i)),
            pl.BlockSpec((samples, batch), lambda i: (0, 0)),
            pl.BlockSpec((samples, batch), lambda i: (0, 0)),
        ],
        out_specs=[
            pl.BlockSpec((samples, blk), lambda i: (0, i)),
            pl.BlockSpec((samples, blk), lambda i: (0, i)),
        ],
        out_shape=[jax.ShapeDtypeStruct((samples, count), F32)] * 2,
        scratch_shapes=[
            pltpu.VMEM((2, batch, WIDE), BF16),
            pltpu.VMEM((2, 2 * samples, batch), BF16),
            pltpu.VMEM((blk // WIDE * 2 * samples, batch), BF16),
        ],
        compiler_params=params(),
        cost_estimate=pl.CostEstimate(
            flops=5 * 10**9, bytes_accessed=4 * samples * count * 4, transcendentals=0
        ),
        name="update",
    )(start, index, coeffs, velocity, grad0, grad1)


def scatter_sum(tiles, axes):
    return jnp.sum(lax.all_to_all(tiles, axes, 0, 0, tiled=True), axis=0)


def gather_all(tile, axes, size):
    copies = jnp.broadcast_to(tile[None], (size,) + tile.shape)
    return lax.all_to_all(copies, axes, 0, 0, tiled=True)


def from_tiles(tiles):
    i, j, high, wide = tiles.shape
    return tiles.transpose(0, 2, 1, 3).reshape(i * high, j * wide)


def after(value, *others):
    return lax.optimization_barrier((value,) + others)[0]


def per_device(n_rows, n_cols, points, coeffs, velocity, targets, batch_index, test_points):
    feats, count = points.shape
    samples = coeffs.shape[0]
    _, batch = batch_index.shape
    devices = n_rows * n_cols
    start = (lax.axis_index(BOTH) * count).astype(jnp.int32).reshape(1)
    blocks = batch_index.reshape(-1, 1, 512)

    mine = gather_points(start, blocks, points)
    test_mine = from_tiles_in(test_points)
    tests = gather_all(test_mine, "cols", n_cols)
    tests = tests.reshape(n_cols, 2, -1, 8, 128).transpose(1, 3, 0, 2, 4).reshape(feats, -1)
    sides, halves = prepare(points, coeffs, velocity)
    part = scatter_sum(mine.reshape(devices, 4, 128), BOTH)
    terms = gather_terms(start, blocks, coeffs, velocity, targets)
    test_part = test_sums(0, n_cols, tests, sides, halves, None)
    test_part = after(test_part, part, terms)
    drawn = gather_all(part, BOTH, devices)
    test_part = test_sums(1, n_cols, tests, sides, halves, test_part)
    drawn = after(drawn, test_part)
    drawn = from_tiles(drawn.reshape(mine.shape))

    sums = batch_sums(drawn, sides, halves, terms)
    test_part = after(test_part, sums)
    part = scatter_sum(sums.reshape(devices, 8, 128), BOTH)
    test_part = test_sums(2, n_cols, tests, sides, halves, test_part)
    test_part = after(test_part, part)
    sums = gather_all(part, BOTH, devices)
    test_part = test_sums(3, n_cols, tests, sides, halves, test_part)
    sums = from_tiles(sums.reshape(samples // 8, -1, 8, 128))
    grad0 = sums[:, :batch]

    test_part = scatter_sum(test_part.reshape(devices, 8, 128), BOTH)
    grad1 = second_gradient(drawn, batch_index, blocks, grad0, sums[:, batch:])
    change = test_change(test_points, drawn, grad0, grad1)
    coeffs_out, velocity_out = update(start, batch_index, coeffs, velocity, grad0, grad1)
    slab = gather_all(test_part, "rows", n_rows)
    slab = from_tiles(slab.reshape(samples // 8, -1, 8, 128)) + change
    return (coeffs_out, velocity_out, slab)


def from_tiles_in(x):
    rows, columns = x.shape
    return (
        x.reshape(rows // 8, 8, columns // 128, 128).transpose(0, 2, 1, 3).reshape(-1, 8, 128)
    )


def solution(mesh):
    n_rows, n_cols = mesh.shape["rows"], mesh.shape["cols"]
    return jax.shard_map(
        functools.partial(per_device, n_rows, n_cols),
        mesh=mesh,
        in_specs=(
            P(None, BOTH),
            P(None, BOTH),
            P(None, BOTH),
            P(None, BOTH),
            P(),
            P(None, "cols"),
        ),
        out_specs=(P(None, BOTH), P(None, BOTH), P(None, "cols")),
        check_vma=False,
    )
```

time: 1100 us -> 232 us (0.21)
  waiting for transfers between devices: 484 us -> 15.1 us
  matrix products: 419 us -> 0 us
  Pallas kernels: 0 us -> 123 us
  local copies, waits for them, and re-layouts: 87.6 us -> 24.3 us
  other arithmetic: 63.9 us -> 1.1 us
  starting transfers between devices: 0.46 us -> 43.4 us
  between operations: 14.2 us -> 0.91 us
    psum x4 -> x0, waiting for transfers between devices: 463 us -> none  [the longest x2 261 us: per_device(): gradient = lax.psum(partial_sums + own_terms, ('rows', 'cols'))]
    dot_general x32 -> x0, matrix products: 419 us -> none  [the longest x16 372 us: matern_tile(): jnp.dot(points_block.T, queries, precision=lax.Precision.HIGHEST, preferr...]
    pallas_call x0 -> x11, Pallas kernels: none -> 123 us  [the longest x1 41.5 us: batch_sums(): pl.pallas_call(batch_kernel, grid=(steps,), in_specs=[pl.BlockSpec((feats...]
    gather x6 -> x0, local copies, waits for them, and re-layouts: 58.9 us -> none  [take_owned(): return jnp.take(array, safe_rows, axis=1) * weights[None, :]]
    all_to_all x0 -> x6, starting transfers between devices: none -> 43.4 us  [the longest x4 22.2 us: gather_all(): return lax.all_to_all(copies, axes, 0, 0, tiled=True)]
    scatter-add x2 -> x0, other arithmetic: 31.5 us -> none  [per_device(): jnp.zeros_like(coeffs_now).at[:, safe_rows].add(gradient * weights[None, :])]
    all_to_all x0 -> x1, blocking collectives: none -> 22.8 us  [scatter_sum(): return jnp.sum(lax.all_to_all(tiles, axes, 0, 0, tiled=True), axis=0)]
    reduce_scatter x1 -> x0, waiting for transfers between devices: 20.8 us -> none  [per_device(): lax.psum_scatter(partial_test, 'cols', scatter_dimension=1, tiled=True)]
  transfers between devices with their start and end apart: 5 -> 6, of which waited for: 5 -> 2; matrix products, arithmetic and copies ran while one was open for 5% -> 0% of each run, Pallas kernels for 0% -> 31%
where the time goes in v1:
time: 232 us; the launch traced here: 231 us
  Pallas kernels  123 us (53%)
  starting transfers between devices  43.4 us (19%)
  local copies, waits for them, and re-layouts  24.3 us (10%)
  blocking collectives  22.8 us (10%)
  waiting for transfers between devices  15.1 us (7%)
    pallas_call x1, Pallas kernels, batch_sums(): pl.pallas_call(batch_kernel, grid=(steps,), in_specs=[pl.BlockSpec((feats...  41.5 us
    pallas_call x4, Pallas kernels, test_sums(): pl.pallas_call(test_kernel, grid=(steps,), in_specs=in_specs, out_specs=p...  40.9 us
    all_to_all x1, blocking collectives, scatter_sum(): return jnp.sum(lax.all_to_all(tiles, axes, 0, 0, tiled=True), axis=0)  22.8 us
    all_to_all x4, starting transfers between devices, gather_all(): return lax.all_to_all(copies, axes, 0, 0, tiled=True)  22.2 us
    all_to_all x2, starting transfers between devices, scatter_sum(): return jnp.sum(lax.all_to_all(tiles, axes, 0, 0, tiled=True), axis=0)  21.2 us
    unnamed x39, local copies, waits for them, and re-layouts  19.6 us
    all_to_all x4, waiting for transfers between devices, gather_all(): return lax.all_to_all(copies, axes, 0, 0, tiled=True)  14.2 us
    pallas_call x1, Pallas kernels, second_gradient(): pl.pallas_call(second_kernel, grid=(steps,), in_specs=[pl.BlockSpec((feat...  10 us
  transfers between devices with their start and end apart: 6, of which 2 were waited for; matrix products, arithmetic and copies ran while one was open for 0% of the time, Pallas kernels for 31%

profile of v1, /device:TPU:1, one launch (start us, length us, event | category | flops | bytes accessed | tf_op | source)
XLA Modules:
  0.0 231.0 jit_solution(15531940463512887398)
XLA Ops:
  0.6 0.0 copy-start
  0.6 1.6 broadcast_in_dim.12
  2.3 4.8 %all-to-all-start.2 = ((f32[4,16,8,128]{3,2,1,0:T(8,128)}), f32[4,16,8,128]{3,2,1,0:T(8,128)S(1)}, u32[]{:S(2)}, u32[]{:S(2)}) async-start(f32[4,16,8,128]{3,2,1,0:T(8,128)} %broadcast_in_dim.12), calls=%async_computation.2 | async-start | bytes 524288 | tf_op jit(solution)/shard_map/all_to_all | solution.py:490
  7.1 0.7 reshape.53.index.index1
  7.9 0.0 copy-start.3
  7.9 1.0 copy-done.3
  8.9 5.5 %gather_points.1 = f32[4,32,4,128]{3,2,1,0:T(4,128)} custom-call(s32[1]{0:T(128)} %bitcast.start, s32[8,1,512]{2,1,0:T(1,128)S(1)} %reshape.53.index.index1, f32[16,8192]{1,0:T(8,128)S(1)} %copy-done.3), custom_call_target="tpu_custom_call" | custom-call | tf_op jit(solution)/shard_map/gather_points/pallas_call | solution.py:162
  14.5 0.0 copy-done
  14.5 0.0 copy-start.1
  14.5 1.2 copy-done.1
  15.7 0.0 copy-start.4
  15.7 1.0 copy-done.4
  16.7 3.3 %prepare.1 = (bf16[128,8192]{1,0:T(8,128)(2,1)}, bf16[3,32,8192]{2,1,0:T(8,128)(2,1)S(1)}) custom-call(f32[16,8192]{1,0:T(8,128)S(1)} %copy-done.4, f32[32,8192]{1,0:T(8,128)S(1)} %copy-done, f32[32,8192]{1,0:T(8,128)S(1)} %copy-done.1), custom_call_target="tpu_custom_call" | custom-call | tf_op jit(solution)/shard_map/prepare/pallas_call | solution.py:105
  20.0 1.1 copy-done.13
  21.2 0.0 copy-done.5
  21.2 6.4 %gather_terms.1.terms = f32[4,32,8,128]{3,2,1,0:T(8,128)S(1)} custom-call(s32[1]{0:T(128)} %bitcast.start, s32[8,1,512]{2,1,0:T(1,128)S(1)} %reshape.53.index.index1, f32[32,8192]{1,0:T(8,128)S(1)} %copy-done, f32[32,8192]{1,0:T(8,128)S(1)} %copy-done.1, f32[32,8192]{1,0:T(8,128)S(1)} %copy-done.5), custom_call_target="tpu_custom_call" | custom-call | tf_op jit(solution)/shard_map/gather_terms/pallas_call | solution.py:202
  27.6 0.0 all-to-all-done.2
  27.6 11.5 %all-to-all-start = ((f32[128,4,128]{2,1,0:T(4,128)}), f32[128,4,128]{2,1,0:T(4,128)S(1)}, u32[]{:S(2)}, u32[]{:S(2)}) async-start(f32[128,4,128]{2,1,0:T(4,128)} %bitcast.1), calls=%async_computation | async-start | bytes 524288 | tf_op jit(solution)/shard_map/all_to_all | solution.py:485
  39.1 0.0 copy-start.8
  39.1 1.6 copy-done.8
  40.7 1.4 copy-done.14
  42.1 10.2 %test_sums.4.refs_0_ = f32[4,8,4,8,128]{4,3,2,1,0:T(8,128)S(1)} custom-call(f32[16,4096]{1,0:T(8,128)S(1)} %bitcast.36, bf16[128,8192]{1,0:T(8,128)(2,1)S(1)} %copy-done.8, bf16[3,32,8192]{2,1,0:T(8,128)(2,1)S(1)} %copy-done.14), custom_call_target="tpu_custom_call" | custom-call | flops 8589934592 | bytes 1048576 | tf_op jit(solution)/shard_map/test_sums/pallas_call | solution.py:292
  52.4 0.0 all-to-all-done
  52.4 0.1 reduce_sum.27
  52.5 0.7 broadcast_in_dim.10
  53.2 9.8 %all-to-all-start.1 = ((f32[128,4,128]{2,1,0:T(4,128)}), f32[128,4,128]{2,1,0:T(4,128)S(1)}, u32[]{:S(2)}, u32[]{:S(2)}) async-start(f32[128,4,128]{2,1,0:T(4,128)} %broadcast_in_dim.10), calls=%async_computation.1 | async-start | bytes 524288 | tf_op jit(solution)/shard_map/all_to_all | solution.py:490
  63.0 0.0 copy-start.9
  63.0 1.6 copy-done.9
  64.6 1.4 copy-done.15
  66.0 10.2 %test_sums.5.refs_0_ = f32[4,8,4,8,128]{4,3,2,1,0:T(8,128)S(1)} custom-call(f32[16,4096]{1,0:T(8,128)S(1)} %bitcast.37, bf16[128,8192]{1,0:T(8,128)(2,1)S(1)} %copy-done.9, bf16[3,32,8192]{2,1,0:T(8,128)(2,1)S(1)} %copy-done.15, f32[4,8,4,8,128]{4,3,2,1,0:T(8,128)S(1)} %test_sums.4.refs_0_), custom_call_target="tpu_custom_call", output_to_operand_aliasing={{}: (3, {})} | custom-call | flops 8589934592 | bytes 1048576 | tf_op jit(solution)/shard_map/test_sums/pallas_call | solution.py:292
  76.2 0.0 all-to-all-done.1
  76.3 0.2 copy.19
  76.5 0.0 copy-start.10
  76.5 1.6 copy-done.10
  78.1 1.4 copy-done.16
  79.5 41.5 %batch_sums.1 = f32[4,32,8,128]{3,2,1,0:T(8,128)} custom-call(f32[16,4096]{1,0:T(8,128)S(1)} %bitcast.32, bf16[128,8192]{1,0:T(8,128)(2,1)S(1)} %copy-done.10, bf16[3,32,8192]{2,1,0:T(8,128)(2,1)S(1)} %copy-done.16, f32[4,32,8,128]{3,2,1,0:T(8,128)S(1)} %gather_terms.1.terms), custom_call_target="tpu_custom_call" | custom-call | flops 34359738368 | bytes 1048576 | tf_op jit(solution)/shard_map/batch_sums/pallas_call | solution.py:250
  121.0 9.8 %all-to-all-start.3 = ((f32[128,8,128]{2,1,0:T(8,128)}), f32[128,8,128]{2,1,0:T(8,128)S(1)}, u32[]{:S(2)}, u32[]{:S(2)}) async-start(f32[128,8,128]{2,1,0:T(8,128)} %bitcast.10), calls=%async_computation.3 | async-start | bytes 1048576 | tf_op jit(solution)/shard_map/all_to_all | solution.py:485
  130.8 0.0 copy-start.11
  130.8 1.6 copy-done.11
  132.4 1.4 copy-done.17
  133.8 10.2 %test_sums.6.refs_0_ = f32[4,8,4,8,128]{4,3,2,1,0:T(8,128)S(1)} custom-call(f32[16,4096]{1,0:T(8,128)S(1)} %bitcast.38, bf16[128,8192]{1,0:T(8,128)(2,1)S(1)} %copy-done.11, bf16[3,32,8192]{2,1,0:T(8,128)(2,1)S(1)} %copy-done.17, f32[4,8,4,8,128]{4,3,2,1,0:T(8,128)S(1)} %test_sums.5.refs_0_), custom_call_target="tpu_custom_call", output_to_operand_aliasing={{}: (3, {})} | custom-call | flops 8589934592 | bytes 1048576 | tf_op jit(solution)/shard_map/test_sums/pallas_call | solution.py:292
  144.0 0.9 all-to-all-done.3
  144.9 0.1 reduce_sum.28
  145.0 1.6 copy-done.12
  146.6 1.4 copy-done.18
  148.0 10.2 %test_sums.7 = f32[4,8,4,8,128]{4,3,2,1,0:T(8,128)S(1)} custom-call(f32[16,4096]{1,0:T(8,128)S(1)} %bitcast.39, bf16[128,8192]{1,0:T(8,128)(2,1)S(1)} %copy-done.12, bf16[3,32,8192]{2,1,0:T(8,128)(2,1)S(1)} %copy-done.18, f32[4,8,4,8,128]{4,3,2,1,0:T(8,128)S(1)} %test_sums.6.refs_0_), custom_call_target="tpu_custom_call", output_to_operand_aliasing={{}: (3, {})} | custom-call | flops 8589934592 | bytes 1048576 | tf_op jit(solution)/shard_map/test_sums/pallas_call | solution.py:292
  158.3 0.0 copy-start.7
  158.3 22.8 %all_to_all.35 = f32[128,8,128]{2,1,0:T(8,128)S(1)} all-to-all(f32[128,8,128]{2,1,0:T(8,128)S(1)} %bitcast.31), channel_id=1, replica_groups=mesh['rows'=32,'cols'=4] {'rows','cols'}, dimensions={0} | all-to-all | bytes 1048576 | tf_op jit(solution)/shard_map/all_to_all | solution.py:485
  181.1 0.8 broadcast_in_dim.13
  181.9 3.6 %all-to-all-start.4 = ((f32[128,8,128]{2,1,0:T(8,128)}), f32[128,8,128]{2,1,0:T(8,128)S(1)}, u32[]{:S(2)}, u32[]{:S(2)}) async-start(f32[128,8,128]{2,1,0:T(8,128)} %broadcast_in_dim.13), calls=%async_computation.4 | async-start | bytes 1048576 | tf_op jit(solution)/shard_map/all_to_all | solution.py:490
  185.6 0.1 reduce_sum.29
  185.7 14.1 %all-to-all-done.4 = f32[128,8,128]{2,1,0:T(8,128)S(1)} async-done(((f32[128,8,128]{2,1,0:T(8,128)}), f32[128,8,128]{2,1,0:T(8,128)S(1)}, u32[]{:S(2)}, u32[]{:S(2)}) %all-to-all-start.4) | async-done | bytes 524320 | tf_op jit(solution)/shard_map/all_to_all | solution.py:490
  199.9 0.7 broadcast_in_dim.14
  200.5 4.0 %all-to-all-start.6 = ((f32[32,8,128]{2,1,0:T(8,128)}), f32[32,8,128]{2,1,0:T(8,128)S(1)}, u32[]{:S(2)}, u32[]{:S(2)}) async-start(f32[32,8,128]{2,1,0:T(8,128)} %broadcast_in_dim.14), calls=%async_computation.6 | async-start | bytes 262144 | tf_op jit(solution)/shard_map/all_to_all | solution.py:490
  204.5 0.0 copy-done.7
  204.5 0.0 copy-start.2
  204.5 10.0 %second_gradient.1.grad1 = f32[32,2048]{1,0:T(8,128)S(1)} custom-call(f32[16,4096]{1,0:T(8,128)S(1)} %bitcast.33, f32[16,4096]{1,0:T(8,128)S(1)} %bitcast.34, s32[2,2048]{1,0:T(2,128)S(1)} %copy-done.7, s32[8,1,512]{2,1,0:T(1,128)S(1)} %reshape.53.index.index1, f32[32,2048]{1,0:T(8,128)S(1)} %get-tuple-element.20.grad.grad0, ...), custom_call_target="tpu_custom_call" | custom-call | flops 4294967296 | bytes 1048576 | tf_op jit(solution)/shard_map/second_gradient/pallas_call | solution.py:340
  214.6 0.0 copy-done.2
  214.6 0.0 copy-start.6
  214.6 6.8 %update.1 = (f32[32,8192]{1,0:T(8,128)}, f32[32,8192]{1,0:T(8,128)}) custom-call(s32[1]{0:T(128)} %bitcast.start, s32[2,2048]{1,0:T(2,128)S(1)} %copy-done.7, f32[32,8192]{1,0:T(8,128)S(1)} %copy-done, f32[32,8192]{1,0:T(8,128)S(1)} %copy-done.2, f32[32,2048]{1,0:T(8,128)S(1)} %get-tuple-element.20.grad.grad0, f32[32,2048]{1,0:T(8,128)S(1)} %second_gradient.1.grad1), custom_call_target="tpu_custom_call" | custom-call | flops 5000000000 | bytes 4194304 | tf_op jit(solution)/shard_map/update/pallas_call | solution.py:455
  221.3 0.0 copy-done.6
  221.3 8.9 %test_change.1 = f32[32,1024]{1,0:T(8,128)S(1)} custom-call(f32[16,1024]{1,0:T(8,128)S(1)} %copy-done.6, f32[16,4096]{1,0:T(8,128)S(1)} %bitcast.35, f32[32,2048]{1,0:T(8,128)S(1)} %get-tuple-element.20.grad.grad0, f32[32,2048]{1,0:T(8,128)S(1)} %second_gradient.1.grad1), custom_call_target="tpu_custom_call" | custom-call | flops 4294967296 | bytes 1048576 | tf_op jit(solution)/shard_map/test_change/pallas_call | solution.py:386
  230.3 0.0 all-to-all-done.6
  230.3 0.7 add.7
  (12 shorter events, 0.1 us)
Async XLA Ops:
  0.6 13.8 %copy-start = (f32[32,8192]{1,0:T(8,128)S(1)}, f32[32,8192]{1,0:T(8,128)}, u32[]{:S(2)}) copy-start(f32[32,8192]{1,0:T(8,128)} %coeffs.5) | copy-start | bytes 3145732
  2.3 25.3 %all-to-all-start.2 = ((f32[4,16,8,128]{3,2,1,0:T(8,128)}), f32[4,16,8,128]{3,2,1,0:T(8,128)S(1)}, u32[]{:S(2)}, u32[]{:S(2)}) async-start(f32[4,16,8,128]{3,2,1,0:T(8,128)} %broadcast_in_dim.12), calls=%async_computation.2 | async-start | bytes 524288 | tf_op jit(solution)/shard_map/all_to_all | solution.py:490
  7.9 1.0 copy-start.3
  14.5 1.2 copy-start.1
  15.7 1.0 copy-start.4
  16.7 4.5 %copy-start.5 = (f32[32,8192]{1,0:T(8,128)S(1)}, f32[32,8192]{1,0:T(8,128)}, u32[]{:S(2)}) copy-start(f32[32,8192]{1,0:T(8,128)} %targets.1) | copy-start | bytes 3145732
  20.0 1.1 copy-start.13
  27.6 24.7 %all-to-all-start = ((f32[128,4,128]{2,1,0:T(4,128)}), f32[128,4,128]{2,1,0:T(4,128)S(1)}, u32[]{:S(2)}, u32[]{:S(2)}) async-start(f32[128,4,128]{2,1,0:T(4,128)} %bitcast.1), calls=%async_computation | async-start | bytes 524288 | tf_op jit(solution)/shard_map/all_to_all | solution.py:485
  39.1 1.6 copy-start.8
  40.7 1.4 copy-start.14
  53.2 23.0 %all-to-all-start.1 = ((f32[128,4,128]{2,1,0:T(4,128)}), f32[128,4,128]{2,1,0:T(4,128)S(1)}, u32[]{:S(2)}, u32[]{:S(2)}) async-start(f32[128,4,128]{2,1,0:T(4,128)} %broadcast_in_dim.10), calls=%async_computation.1 | async-start | bytes 524288 | tf_op jit(solution)/shard_map/all_to_all | solution.py:490
  63.0 1.6 copy-start.9
  64.6 1.4 copy-start.15
  76.5 1.6 copy-start.10
  78.1 1.4 copy-start.16
  121.0 23.9 %all-to-all-start.3 = ((f32[128,8,128]{2,1,0:T(8,128)}), f32[128,8,128]{2,1,0:T(8,128)S(1)}, u32[]{:S(2)}, u32[]{:S(2)}) async-start(f32[128,8,128]{2,1,0:T(8,128)} %bitcast.10), calls=%async_computation.3 | async-start | bytes 1048576 | tf_op jit(solution)/shard_map/all_to_all | solution.py:485
  130.8 1.6 copy-start.11
  132.4 1.4 copy-start.17
  145.0 1.6 copy-start.12
  146.6 1.4 copy-start.18
  158.3 46.3 %copy-start.7 = (s32[2,2048]{1,0:T(2,128)S(1)}, s32[2,2048]{1,0:T(2,128)}, u32[]{:S(2)}) copy-start(s32[2,2048]{1,0:T(2,128)} %index.1) | copy-start | bytes 49156
  181.9 17.9 %all-to-all-start.4 = ((f32[128,8,128]{2,1,0:T(8,128)}), f32[128,8,128]{2,1,0:T(8,128)S(1)}, u32[]{:S(2)}, u32[]{:S(2)}) async-start(f32[128,8,128]{2,1,0:T(8,128)} %broadcast_in_dim.13), calls=%async_computation.4 | async-start | bytes 1048576 | tf_op jit(solution)/shard_map/all_to_all | solution.py:490
  200.5 29.8 %all-to-all-start.6 = ((f32[32,8,128]{2,1,0:T(8,128)}), f32[32,8,128]{2,1,0:T(8,128)S(1)}, u32[]{:S(2)}, u32[]{:S(2)}) async-start(f32[32,8,128]{2,1,0:T(8,128)} %broadcast_in_dim.14), calls=%async_computation.6 | async-start | bytes 262144 | tf_op jit(solution)/shard_map/all_to_all | solution.py:490
  204.5 10.0 %copy-start.2 = (f32[32,8192]{1,0:T(8,128)S(1)}, f32[32,8192]{1,0:T(8,128)}, u32[]{:S(2)}) copy-start(f32[32,8192]{1,0:T(8,128)} %velocity.5) | copy-start | bytes 3145732
  214.6 6.8 %copy-start.6 = (f32[16,1024]{1,0:T(8,128)S(1)}, f32[16,1024]{1,0:T(8,128)}, u32[]{:S(2)}) copy-start(f32[16,1024]{1,0:T(8,128)} %queries.1) | copy-start | bytes 196612
